TPU v7x, 32 devices: a whole 2x2x4 slice. The times are simulated.
32 devices in a mesh: seq: 8 (over z, x), head: 4 (over y, core).
Axes of the slice: x: 2, y: 2, z: 4, core: 2. Of those that a mesh axis runs over, the one named last changes fastest.
Arguments:
- query_rows: float32 [4096, 1024], P('seq', 'head'), may hold values from -128 to 128
- key_rows: float32 [4096, 1024], P('seq', 'head'), may hold values from -128 to 128
- value_rows: float32 [4096, 1024], P('seq', 'head'), may hold values from -6 to 6
- teacher_out: float32 [4096, 1024], P(('seq', 'head')), may hold values from -6 to 6
- query_map: float32 [4, 256, 256], P('head'), may hold values from -1 to 1
- key_map: float32 [4, 256, 256], P('head'), may hold values from -1 to 1
- block_map: int32 [8, 8], replicated, may hold values from 0 to 63, as said below
Outputs:
- grad_query_map: float32 [4, 256, 256], P('head', 'seq')
- grad_key_map: float32 [4, 256, 256], P('head', 'seq')
Inputs may be any that keep to these rules, and one draw needn't show every extreme that they name: `block_map`: row d lists, slot by slot, the sequence blocks whose teacher rows storage row group d holds (storage block d * 8 + j). Sequence block b belongs to owner b // 8. Every row names exactly one block of each owner, and every block appears exactly once in the table.
All inputs are finite; a program needn't handle non-finite values.
Results may differ from a plain program's by a relative error of at most 0.00035.
Values sent between devices are 32-bit elements; how exact they have to be, the bound alone decides.
A program may use at most 128 MiB of HBM per device.

v0:
```python
import jax
import jax.numpy as jnp
from jax import lax
from jax.sharding import PartitionSpec as P

exact_prec = lax.Precision.HIGHEST


def prefix(value, axis, join, neutral, backward):
    count, mine = (lax.axis_size(axis), lax.axis_index(axis))
    pieces = jax.tree.map(lambda part: lax.all_gather(part, axis), value)
    if backward:
        pieces = jax.tree.map(lambda part: part[::-1], pieces)
        mine = count - 1 - mine
    total = jax.tree.map(
        lambda part, zero: jnp.full_like(part, 0) + jnp.asarray(zero, part.dtype), value, neutral
    )

    def step(position, total):
        longer = join(total, jax.tree.map(lambda part: part[position], pieces))
        return jax.tree.map(lambda new, old: jnp.where(position < mine, new, old), longer, total)

    return lax.fori_loop(0, count - 1, step, total)


def back_pair(first_half, second_half, grad_feat, half_feat):
    grad_first = grad_feat[..., :half_feat]
    grad_second = grad_feat[..., half_feat:]
    lead = first_half * (grad_first - jnp.sum(first_half * grad_first, axis=-1, keepdims=True))
    trail = second_half * (grad_second - jnp.sum(second_half * grad_second, axis=-1, keepdims=True))
    return lead - trail


def add_pair(earlier, later_one):
    return (earlier[0] + later_one[0], earlier[1] + later_one[1])


def relay_teacher(teacher_out, block_map):
    gathered = lax.all_to_all(teacher_out, "head", split_axis=1, concat_axis=0, tiled=True)
    seq_count = lax.axis_size("seq")
    position = lax.axis_index("seq")
    columns = gathered.shape[1]
    block_rows = gathered.shape[0] // seq_count
    blocks = gathered.reshape(seq_count, block_rows, columns)
    slot_ids = lax.dynamic_index_in_dim(block_map, position, 0, keepdims=False)
    owner_ids = slot_ids // seq_count
    ladder = jnp.arange(seq_count, dtype=jnp.int32)
    to_owner = (owner_ids[None, :] == ladder[:, None]).astype(jnp.float32)
    by_owner = jnp.einsum("oj,jrc->orc", to_owner, blocks, precision=exact_prec)
    arrived = lax.all_to_all(by_owner, "seq", split_axis=0, concat_axis=0, tiled=True)
    own_mask = block_map // seq_count == position
    within = jnp.sum(jnp.where(own_mask, block_map % seq_count, 0), axis=1)
    placing = (within[None, :] == ladder[:, None]).astype(jnp.float32)
    placed = jnp.einsum("is,src->irc", placing, arrived, precision=exact_prec)
    return placed.reshape(seq_count * block_rows, columns)


def per_device(query_rows, key_rows, value_rows, teacher_out, query_map, key_map, block_map):
    tokens = query_rows.shape[0]
    local_heads = query_map.shape[0]
    head_width = query_map.shape[1]
    half_feat = query_map.shape[2]
    queries = query_rows.reshape(tokens, local_heads, head_width).transpose(1, 0, 2)
    keys_h = key_rows.reshape(tokens, local_heads, head_width).transpose(1, 0, 2)
    values_h = value_rows.reshape(tokens, local_heads, head_width).transpose(1, 0, 2)
    pre_q = jnp.einsum("hte,hef->htf", queries, query_map, precision=exact_prec)
    pre_k = jnp.einsum("hte,hef->htf", keys_h, key_map, precision=exact_prec)
    first_q = jax.nn.softmax(pre_q, axis=-1)
    second_q = jax.nn.softmax(-pre_q, axis=-1)
    first_k = jax.nn.softmax(pre_k, axis=-1)
    second_k = jax.nn.softmax(-pre_k, axis=-1)
    feat_q = jnp.concatenate([first_q, second_q], axis=-1)
    feat_k = jnp.concatenate([first_k, second_k], axis=-1)
    own_state = jnp.einsum("htf,hte->hfe", feat_k, values_h, precision=exact_prec)
    own_norm = jnp.sum(feat_k, axis=1)
    zero_pair = (jnp.zeros_like(own_state), jnp.zeros_like(own_norm))
    prev_state, prev_norm = prefix((own_state, own_norm), "seq", add_pair, zero_pair, False)
    ladder = jnp.arange(tokens, dtype=jnp.int32)
    causal = (ladder[:, None] >= ladder[None, :]).astype(jnp.float32)
    scores = jnp.einsum("htf,hsf->hts", feat_q, feat_k, precision=exact_prec) * causal
    numerator = jnp.einsum("hts,hse->hte", scores, values_h, precision=exact_prec)
    numerator = numerator + jnp.einsum("htf,hfe->hte", feat_q, prev_state, precision=exact_prec)
    raw_sum = jnp.sum(scores, axis=-1) + jnp.einsum(
        "htf,hf->ht", feat_q, prev_norm, precision=exact_prec
    )
    divisor = jnp.maximum(raw_sum, 1.0)
    student = numerator / divisor[..., None]
    teacher_rows = relay_teacher(teacher_out, block_map)
    teacher = teacher_rows.reshape(tokens, local_heads, head_width).transpose(1, 0, 2)
    mismatch = student - teacher
    grad_num = mismatch / divisor[..., None]
    grad_div = jnp.where(raw_sum > 1.0, -jnp.sum(mismatch * student, axis=-1) / divisor, 0.0)
    own_back = jnp.einsum("htf,hte->hfe", feat_q, grad_num, precision=exact_prec)
    own_back_norm = jnp.einsum("ht,htf->hf", grad_div, feat_q, precision=exact_prec)
    next_state, next_norm = prefix((own_back, own_back_norm), "seq", add_pair, zero_pair, True)
    weights = (
        jnp.einsum("hte,hse->hts", grad_num, values_h, precision=exact_prec) + grad_div[..., None]
    ) * causal
    grad_fq = jnp.einsum("hts,hsf->htf", weights, feat_k, precision=exact_prec)
    grad_fq = grad_fq + jnp.einsum("hte,hfe->htf", grad_num, prev_state, precision=exact_prec)
    grad_fq = grad_fq + grad_div[..., None] * prev_norm[:, None, :]
    grad_fk = jnp.einsum("hts,htf->hsf", weights, feat_q, precision=exact_prec)
    grad_fk = grad_fk + jnp.einsum("hse,hfe->hsf", values_h, next_state, precision=exact_prec)
    grad_fk = grad_fk + next_norm[:, None, :]
    grad_pq = back_pair(first_q, second_q, grad_fq, half_feat)
    grad_pk = back_pair(first_k, second_k, grad_fk, half_feat)
    term_q = jnp.einsum("hte,htf->ehf", queries, grad_pq, precision=exact_prec)
    term_k = jnp.einsum("hte,htf->ehf", keys_h, grad_pk, precision=exact_prec)
    summed = lax.psum_scatter(
        jnp.stack([term_q, term_k], axis=1), "seq", scatter_dimension=0, tiled=True
    )
    grad_query = summed[:, 0].transpose(1, 0, 2)
    grad_key = summed[:, 1].transpose(1, 0, 2)
    return (grad_query, grad_key)


def solution(mesh):
    placed = (
        P("seq", "head"),
        P("seq", "head"),
        P("seq", "head"),
        P(("seq", "head"), None),
        P("head", None, None),
        P("head", None, None),
        P(),
    )
    return jax.shard_map(
        per_device,
        mesh=mesh,
        in_specs=placed,
        out_specs=(P("head", "seq", None), P("head", "seq", None)),
        check_vma=False,
    )
```

profile of v0, /device:TPU:0, one launch (start us, length us, event | category | flops | bytes accessed | tf_op | source)
XLA Modules:
  0.0 280.4 jit_solution(3625305701671701663)
XLA Ops:
  7.2 1.8 fusion.73
  9.1 1.8 fusion.74
  11.6 1.8 fusion.9
  14.5 4.2 %all-to-all-start = ((f32[128,4,256]{0,2,1:T(8,128)}), f32[128,4,256]{0,2,1:T(8,128)S(1)}, u32[]{:S(2)}, u32[]{:S(2)}) async-start(f32[128,4,256]{0,2,1:T(8,128)} %bitcast.147), calls=%async_computation | async-start | bytes 1048576 | tf_op jit(solution)/shard_map/all_to_all | solution.py:39
  18.7 8.8 %all-to-all-done = f32[128,4,256]{0,2,1:T(8,128)S(1)} async-done(((f32[128,4,256]{0,2,1:T(8,128)}), f32[128,4,256]{0,2,1:T(8,128)S(1)}, u32[]{:S(2)}, u32[]{:S(2)}) %all-to-all-start) | async-done | bytes 524320 | tf_op jit(solution)/shard_map/all_to_all | solution.py:39
  28.6 1.7 fusion.19
  31.3 6.5 %all-to-all-start.1 = ((f32[8,64,256]{2,1,0:T(8,128)}), f32[8,64,256]{2,1,0:T(8,128)}, u32[]{:S(2)}, u32[]{:S(2)}) async-start(f32[8,64,256]{2,1,0:T(8,128)} %copy.36), calls=%async_computation.1 | async-start | bytes 1048576 | tf_op jit(solution)/shard_map/all_to_all | solution.py:50
  37.9 38.3 %all-gather.4 = f32[8,1,512]{2,1,0:T(1,128)S(1)} all-gather(f32[1,1,512]{2,1,0:T(1,128)S(1)} %bitcast.156), channel_id=3, replica_groups=mesh['seq'=8,'head'=4] {'seq'}, dimensions={0}, use_global_device_ids=true | all-gather | bytes 18432 | tf_op jit(solution)/shard_map/all_gather | solution.py:11
  76.4 1.9 fusion.75
  78.3 1.9 fusion.76
  80.2 1.7 fusion.17
  83.1 13.8 %all-gather.9.cloned.1.call-done = f32[4096,256]{1,0:T(8,128)} async-done(((f32[512,256]{1,0:T(8,128)}), f32[4096,256]{1,0:T(8,128)}) %all-gather.9.cloned.1.call-update) | async-done | bytes 4194320 | tf_op jit(solution)/shard_map/all_gather | solution.py:11
  96.9 8.8 %while.32 = (s32[]{:T(128)}, f32[1,512,256]{2,1,0:T(8,128)S(1)}, f32[1,512]{1,0:T(1,128)S(1)}, s32[]{:T(128)}, f32[8,1,512,256]{3,2,1,0:T(8,128)}, /*index=5*/f32[8,1,512]{2,1,0:T(1,128)S(1)}, s32[]{:T(128)}, s32[]{:T(128)}) while((s32[]{:T(128)}, f32[1,512,256]{2,1,0:T(8,128)S(1)}, f32[1,512]{1,0:T(1,128)S(1)}, s32[]{:T(128)}, ...), condition=%wide.region_10.11_spmd.clone, body=%wide.region_9.10_spmd.clone.sunk | while | flops 394756 | bytes 1579123 | solution.py:23
  106.4 2.2 multiply_reduce_fusion.4
  109.4 1.8 fusion.48
  112.3 26.7 %all-gather.5 = f32[8,1,512]{2,1,0:T(1,128)S(1)} all-gather(f32[1,1,512]{2,1,0:T(1,128)S(1)} %convolution_bitcast_fusion.3), channel_id=5, replica_groups=mesh['seq'=8,'head'=4] {'seq'}, dimensions={0}, use_global_device_ids=true | all-gather | bytes 18432 | tf_op jit(solution)/shard_map/all_gather | solution.py:11
  139.0 2.2 fusion.5
  141.1 3.0 %fusion.7 = f32[512,512]{0,1:T(8,128)S(1)} fusion(f32[512,512]{0,1:T(8,128)S(1)} %fusion.5, f32[1,512,256]{1,2,0:T(8,128)} %copy-done.1, f32[1,512,256]{1,2,0:T(8,128)S(1)} %get-tuple-element.342), kind=kOutput, calls=%fused_computation.23 | convolution fusion | flops 1610874880 | bytes 3145728 | tf_op jit(solution)/shard_map/hts,hsf->htf/dot_general | solution.py:99
  146.1 2.9 %fusion.49 = f32[512,512]{0,1:T(8,128)} fusion(f32[512,512]{0,1:T(8,128)S(1)} %fusion.5, f32[1,512,256]{1,2,0:T(8,128)S(1)} %get-tuple-element.348, f32[1,512,256]{1,2,0:T(8,128)S(1)} %get-tuple-element.349), kind=kOutput, calls=%fused_computation.83 | convolution fusion | flops 1610874880 | bytes 3145728 | tf_op jit(solution)/shard_map/hts,htf->hsf/dot_general | solution.py:102
  149.1 34.2 %all-gather.11.cloned.1.call-done = f32[4096,256]{1,0:T(8,128)} async-done(((f32[512,256]{1,0:T(8,128)}), f32[4096,256]{1,0:T(8,128)}) %all-gather.11.cloned.1.call-update) | async-done | bytes 4194320 | tf_op jit(solution)/shard_map/all_gather | solution.py:11
  183.3 4.5 %rev.6 = f32[8,1,512,256]{3,2,1,0:T(8,128)} reverse(f32[8,1,512,256]{3,2,1,0:T(8,128)} %bitcast.145), dimensions={0} | reverse | bytes 8388608 | tf_op jit(solution)/shard_map/rev | solution.py:13
  187.7 8.8 %while.33 = (s32[]{:T(128)}, f32[1,512,256]{2,1,0:T(8,128)S(1)}, f32[1,512]{1,0:T(1,128)S(1)}, s32[]{:T(128)}, f32[8,1,512,256]{3,2,1,0:T(8,128)}, /*index=5*/f32[8,1,512]{2,1,0:T(1,128)S(1)}, s32[]{:T(128)}, s32[]{:T(128)}) while((s32[]{:T(128)}, f32[1,512,256]{2,1,0:T(8,128)S(1)}, f32[1,512]{1,0:T(1,128)S(1)}, s32[]{:T(128)}, ...), condition=%wide.region_17.18_spmd.clone, body=%wide.region_16.17_spmd.clone.sunk | while | flops 394756 | bytes 1579123 | solution.py:23
  196.5 2.3 fusion.2
  202.1 69.5 %all-reduce.3.cloned.1.call-done = f32[256,2,1,256]{3,1,2,0:T(2,128)} async-done(((f32[256,2,1,256]{3,1,2,0:T(2,128)}), f32[256,2,1,256]{3,1,2,0:T(2,128)}) %all-reduce.3.cloned.1.call-update) | async-done | bytes 524304
  (88 shorter events, 31.7 us)
Async XLA Ops:
  7.2 4.5 %copy-start = (f32[512,256]{1,0:T(8,128)S(1)}, f32[512,256]{1,0:T(8,128)}, u32[]{:S(2)}) copy-start(f32[512,256]{1,0:T(8,128)} %param.13) | copy-start | bytes 1572868
  7.2 89.7 %all-gather.9.cloned.1.call-start = ((), (), s32[]{:S(2)}) async-start(), calls=%async_computation.2 | async-start | bytes 4718592 | tf_op jit(solution)/shard_map/all_gather | solution.py:11
  9.1 4.4 %copy-start.7 = (f32[128,1024]{1,0:T(8,128)S(1)}, f32[128,1024]{1,0:T(8,128)}, u32[]{:S(2)}) copy-start(f32[128,1024]{1,0:T(8,128)} %param.14) | copy-start | bytes 1572868
  11.1 7.6 %copy-start.9 = (s32[8,8]{1,0:T(8,128)S(1)}, s32[8,8]{1,0:T(8,128)}, u32[]{:S(2)}) copy-start(s32[8,8]{1,0:T(8,128)} %param.17) | copy-start | bytes 772
  11.6 64.8 %copy-start.1 = (f32[1,512,256]{1,2,0:T(8,128)}, f32[1,512,256]{1,2,0:T(8,128)S(1)}, u32[]{:S(2)}) copy-start(f32[1,512,256]{1,2,0:T(8,128)S(1)} %get-tuple-element.343) | copy-start | bytes 1572868
  14.5 13.1 %all-to-all-start = ((f32[128,4,256]{0,2,1:T(8,128)}), f32[128,4,256]{0,2,1:T(8,128)S(1)}, u32[]{:S(2)}, u32[]{:S(2)}) async-start(f32[128,4,256]{0,2,1:T(8,128)} %bitcast.147), calls=%async_computation | async-start | bytes 1048576 | tf_op jit(solution)/shard_map/all_to_all | solution.py:39
  31.3 49.0 %all-to-all-start.1 = ((f32[8,64,256]{2,1,0:T(8,128)}), f32[8,64,256]{2,1,0:T(8,128)}, u32[]{:S(2)}, u32[]{:S(2)}) async-start(f32[8,64,256]{2,1,0:T(8,128)} %copy.36), calls=%async_computation.1 | async-start | bytes 1048576 | tf_op jit(solution)/shard_map/all_to_all | solution.py:50
  37.7 145.6 %all-gather.11.cloned.1.call-start = ((), (), s32[]{:S(2)}) async-start(), calls=%async_computation.3 | async-start | bytes 4718592 | tf_op jit(solution)/shard_map/all_gather | solution.py:11
  96.9 9.4 %copy-start.8 = (f32[512,256]{0,1:T(8,128)S(1)}, f32[512,256]{0,1:T(8,128)}, u32[]{:S(2)}) copy-start(f32[512,256]{0,1:T(8,128)} %copy.39) | copy-start | bytes 1572868
  108.6 0.8 copy-start.3
  111.2 160.4 %all-reduce.3.cloned.1.call-start = ((), (), s32[]{:S(2)}) async-start(), calls=%async_computation.4 | async-start | bytes 1048576
  139.0 5.2 %copy-start.4 = (f32[512,256]{0,1:T(8,128)S(1)}, f32[512,256]{0,1:T(8,128)}, u32[]{:S(2)}) copy-start(f32[512,256]{0,1:T(8,128)} %copy-done.3) | copy-start | bytes 1572868
  141.1 4.3 %copy-start.5 = (f32[512,256]{1,0:T(8,128)S(1)}, f32[512,256]{1,0:T(8,128)}, u32[]{:S(2)}) copy-start(f32[512,256]{1,0:T(8,128)} %param.11) | copy-start | bytes 1572868
  187.7 11.1 %copy-start.2 = (f32[1,512,256]{1,2,0:T(8,128)S(1)}, f32[1,512,256]{1,2,0:T(8,128)}, u32[]{:S(2)}) copy-start(f32[1,512,256]{1,2,0:T(8,128)} %copy-done.1) | copy-start | bytes 1572868
  196.5 2.6 copy-start.6
  198.9 2.0 copy-start.10
Sparse Core Ops, SparseCore 0:
  13.6 83.2 all-gather.8
  111.4 71.8 all-gather.10
  201.0 70.6 all-reduce.2
where the time goes:
time: 282 us; the launch traced here: 280 us
  waiting for transfers between devices  126 us (45%)
  blocking collectives  65 us (23%)
  matrix products  31.1 us (11%)
  other arithmetic  18.7 us (7%)
  between operations  14.7 us (5%)
  local copies, waits for them, and re-layouts  13.3 us (5%)
  starting transfers between devices  10.8 us (4%)
    unnamed x4, waiting for transfers between devices  69.6 us
    all_gather x2, blocking collectives, prefix(): pieces = jax.tree.map(lambda part: lax.all_gather(part, axis), value)  65 us
    all_gather x2, waiting for transfers between devices, prefix(): pieces = jax.tree.map(lambda part: lax.all_gather(part, axis), value)  48 us
    select_n x28, other arithmetic, step(): jnp.where(position < mine, new, old)  17.2 us
    all_to_all x1, waiting for transfers between devices, relay_teacher(): lax.all_to_all(teacher_out, 'head', split_axis=1, concat_axis=0, tiled=True)  8.83 us
    all_to_all x1, starting transfers between devices, relay_teacher(): lax.all_to_all(by_owner, 'seq', split_axis=0, concat_axis=0, tiled=True)  6.46 us
  transfers between devices with their start and end apart: 5, of which 4 were waited for; matrix products, arithmetic and copies ran while one was open for 8% of the time, Pallas kernels for 0%

commit v1 on v0

v1 whole, which is shorter than its diff:
```python
import functools

import jax
import jax.numpy as jnp
from jax import lax
from jax.experimental import pallas as pl
from jax.experimental.pallas import tpu as pltpu
from jax.sharding import PartitionSpec as P

MESH = pl.DeviceIdType.MESH
F32 = jnp.float32
BF16 = jnp.bfloat16
NN = (((1,), (0,)), ((), ()))
NT = (((1,), (1,)), ((), ()))
TN = (((0,), (0,)), ((), ()))


def split(x):
    hi = x.astype(BF16)
    return hi, (x - hi.astype(F32)).astype(BF16)


def dot3(a, b, dims):
    one = functools.partial(
        lax.dot_general, dimension_numbers=dims, preferred_element_type=F32
    )
    return one(a[0], b[0]) + (one(a[0], b[1]) + one(a[1], b[0]))


def chunk_bounds(rows, count):
    units = rows // 8
    edges = [8 * (units * i // count) for i in range(count + 1)]
    return [(edges[i], edges[i + 1] - edges[i]) for i in range(count)]


def kernel(
    n, nh, chunks,
    q_ref, k_ref, v_ref, t_ref, qm_ref, km_ref, bm_ref,
    oq_ref, ok_ref,
    gath, t_send, t_arr, teach,
    vh, vl, fk, fkh, fkl, fq, fqh, fql,
    own, x1, part, chain, give, prev,
    grad_k, terms, rs,
    sem_t1, sem_t2, sem_x1, sem_p, sem_x2, sem_rs, sem_loc,
):
    tokens, width = q_ref.shape
    half = fk.shape[2]
    br = tokens // n
    group = t_ref.shape[0]
    er = width // n
    me = lax.axis_index("seq")
    mh = lax.axis_index("head")
    inner = 2
    outer = n // inner
    z = me // inner
    c = me % inner

    def seq_dev(i):
        return (i, mh)

    barrier = pltpu.get_barrier_semaphore()
    for d in range(1, n):
        pl.semaphore_signal(
            barrier, inc=1, device_id=seq_dev((me + d) % n), device_id_type=MESH
        )
    for d in range(1, nh):
        pl.semaphore_signal(
            barrier, inc=1, device_id=(me, (mh + d) % nh), device_id_type=MESH
        )
    pl.semaphore_wait(barrier, n - 1 + nh - 1)

    def t1_copy(to, frm):
        cols = pl.ds(pl.multiple_of(to * width, 128), width)
        return pltpu.make_async_remote_copy(
            src_ref=t_ref.at[:, cols],
            dst_ref=gath.at[pl.ds(pl.multiple_of(frm * group, 8), group), :],
            send_sem=sem_t1.at[0, to],
            recv_sem=sem_t1.at[1, frm],
            device_id=(me, to),
            device_id_type=MESH,
        )

    for d in range(1, nh):
        t1_copy((mh + d) % nh, mh).start()
    t1_own = pltpu.make_async_copy(
        t_ref.at[:, pl.ds(pl.multiple_of(mh * width, 128), width)],
        gath.at[pl.ds(pl.multiple_of(mh * group, 8), group), :],
        sem_loc.at[0],
    )
    t1_own.start()

    def features(rows_ref, map_ref, f, fh, fl):
        pre = jnp.dot(
            rows_ref[...], map_ref[...], precision=lax.Precision.HIGHEST,
            preferred_element_type=F32,
        )
        up = jnp.exp(pre - jnp.max(pre, axis=-1, keepdims=True))
        p1 = up / jnp.sum(up, axis=-1, keepdims=True)
        down = jnp.exp(jnp.min(pre, axis=-1, keepdims=True) - pre)
        p2 = down / jnp.sum(down, axis=-1, keepdims=True)
        for i, p in enumerate((p1, p2)):
            hi, lo = split(p)
            f[i] = p
            fh[i] = hi
            fl[i] = lo

    partner = seq_dev(z * inner + 1 - c)

    def swap_copy(way, i):
        rows = pl.ds(*chunks[i])
        return pltpu.make_async_remote_copy(
            src_ref=own.at[way, 1 - c, rows], dst_ref=x1.at[way, rows],
            send_sem=sem_x1.at[way, 0, i], recv_sem=sem_x1.at[way, 1, i],
            device_id=partner, device_id_type=MESH,
        )

    def onward_copy(way, i):
        rows = pl.ds(*chunks[i])
        zn = lax.rem(z + (1 if way == 0 else outer - 1), outer)
        return pltpu.make_async_remote_copy(
            src_ref=chain.at[way, rows], dst_ref=part.at[way, rows],
            send_sem=sem_p.at[way, 0, i], recv_sem=sem_p.at[way, 1, i],
            device_id=seq_dev(zn * inner + c), device_id_type=MESH,
        )

    def across_copy(way, i, which):
        rows = pl.ds(*chunks[i])
        return pltpu.make_async_remote_copy(
            src_ref=give.at[way, rows], dst_ref=prev.at[way, which, rows],
            send_sem=sem_x2.at[way, 0, i], recv_sem=sem_x2.at[way, 1, i],
            device_id=partner, device_id_type=MESH,
        )

    def scan_begin(way):
        for i in range(len(chunks)):
            swap_copy(way, i).start()

    def scan_run(way):
        place = z if way == 0 else outer - 1 - z
        leads = (c if way == 0 else 1 - c) == 0

        @pl.when(place == 0)
        def _():
            part[way] = jnp.zeros(part.shape[1:], F32)

        for i in range(len(chunks)):
            at, size = chunks[i]
            rows = pl.ds(at, size)
            swap_copy(way, i).wait_recv()

            @pl.when(place > 0)
            def _():
                onward_copy(way, i).wait_recv()

            @pl.when(place < outer - 1)
            def _():
                chain[way, rows] = part[way, rows] + (own[way, c, rows] + x1[way, rows])
                onward_copy(way, i).start()

            before = part[way, rows]
            give[way, rows] = before + jnp.where(leads, own[way, c, rows], 0.0)
            across_copy(way, i, c).start()
            prev[way, c, rows] = before + jnp.where(leads, 0.0, x1[way, rows])

    def scan_end(way):
        place = z if way == 0 else outer - 1 - z
        for i in range(len(chunks)):
            across_copy(way, i, 1 - c).wait_recv()
            swap_copy(way, i).wait_send()
            across_copy(way, i, c).wait_send()

            @pl.when(place < outer - 1)
            def _():
                onward_copy(way, i).wait_send()

    def put_state(way, which, value, norm):
        own[way, which, 0:width] = value
        own[way, which, width:width + 8] = jnp.broadcast_to(norm, (8, half))

    features(k_ref, km_ref, fk, fkh, fkl)
    v_hi, v_lo = split(v_ref[...])
    vh[...] = v_hi
    vl[...] = v_lo

    def key_state(which):
        put_state(
            0, which,
            dot3((vh[...], vl[...]), (fkh[which], fkl[which]), TN),
            jnp.sum(fk[which], axis=0, keepdims=True),
        )

    key_state(1 - c)
    scan_begin(0)
    key_state(c)

    for d in range(1, nh):
        frm = (mh + d) % nh
        t1_copy(frm, frm).wait_recv()
    t1_own.wait()

    def t2_copy(to, frm):
        return pltpu.make_async_remote_copy(
            src_ref=t_send.at[to],
            dst_ref=t_arr.at[frm],
            send_sem=sem_t2.at[0, to],
            recv_sem=sem_t2.at[1, frm],
            device_id=seq_dev(to),
            device_id_type=MESH,
        )

    mine = bm_ref[pl.ds(me, 1), :]
    for d in range(n):
        to = (me + d) % n
        held = ((mine >= to * n) & (mine < to * n + n)).astype(F32)
        block = jnp.zeros((br, width), F32)
        for j in range(n):
            block = block + held[:, j:j + 1] * gath[j * br:(j + 1) * br]
        if d == 0:
            t_arr[me] = block
        else:
            t_send[to] = block
            t2_copy(to, me).start()

    features(q_ref, qm_ref, fq, fqh, fql)
    causal = (
        lax.broadcasted_iota(jnp.int32, (tokens, tokens), 0)
        >= lax.broadcasted_iota(jnp.int32, (tokens, tokens), 1)
    )
    scores = dot3((fqh[0], fql[0]), (fkh[0], fkl[0]), NT)
    scores = scores + dot3((fqh[1], fql[1]), (fkh[1], fkl[1]), NT)
    scores = jnp.where(causal, scores, 0.0)
    numerator = dot3(split(scores), (vh[...], vl[...]), NN)
    raw_sum = jnp.sum(scores, axis=-1, keepdims=True)

    scan_run(0)
    scan_end(0)

    for i in range(2):
        numerator = numerator + dot3(
            (fqh[i], fql[i]), split(prev[0, i, 0:width]), NT
        )
        raw_sum = raw_sum + jnp.sum(
            fq[i] * prev[0, i, width:width + 1], axis=-1, keepdims=True
        )
    divisor = jnp.maximum(raw_sum, 1.0)
    student = numerator / divisor

    for d in range(1, n):
        frm = (me + d) % n
        t2_copy(frm, frm).wait_recv()
    table = bm_ref[...]
    owned = (table >= me * n) & (table < me * n + n)
    within = jnp.sum(
        jnp.where(owned, table - me * n, 0).astype(F32), axis=1, keepdims=True
    )
    for w in range(n):
        found = (within == w).astype(F32)
        block = jnp.zeros((br, width), F32)
        for s in range(n):
            block = block + found[s:s + 1, :] * t_arr[s]
        teach[w * br:(w + 1) * br] = block

    mismatch = student - teach[...]
    grad_num = mismatch / divisor
    grad_div = jnp.where(
        raw_sum > 1.0,
        -jnp.sum(mismatch * student, axis=-1, keepdims=True) / divisor,
        0.0,
    )
    gn = split(grad_num)

    def query_state(which):
        put_state(
            1, which,
            dot3(gn, (fqh[which], fql[which]), TN),
            jnp.sum(grad_div * fq[which], axis=0, keepdims=True),
        )

    query_state(1 - c)
    scan_begin(1)
    query_state(c)

    weights = dot3(gn, (vh[...], vl[...]), NT) + grad_div
    w_parts = split(jnp.where(causal, weights, 0.0))
    grad_q = []
    for i in range(2):
        g = dot3(w_parts, (fkh[i], fkl[i]), NN)
        g = g + dot3(gn, split(prev[0, i, 0:width]), NN)
        grad_q.append(g + grad_div * prev[0, i, width:width + 1])
        grad_k[i] = dot3(w_parts, (fqh[i], fql[i]), TN)

    def back_pair(f, g1, g2):
        p1, p2 = f[0], f[1]
        lead = p1 * (g1 - jnp.sum(p1 * g1, axis=-1, keepdims=True))
        trail = p2 * (g2 - jnp.sum(p2 * g2, axis=-1, keepdims=True))
        return lead - trail

    def rs_copy(i, to, frm):
        return pltpu.make_async_remote_copy(
            src_ref=terms.at[i, pl.ds(pl.multiple_of(to * er, 8), er), :],
            dst_ref=rs.at[i, frm],
            send_sem=sem_rs.at[i, 0, to],
            recv_sem=sem_rs.at[i, 1, frm],
            device_id=seq_dev(to),
            device_id_type=MESH,
        )

    def rs_begin(i, rows_ref, grad):
        terms[i] = dot3(split(rows_ref[...]), split(grad), TN)
        for d in range(1, n):
            rs_copy(i, (me + d) % n, me).start()

    def rs_finish(i, out_ref):
        total = terms[i, pl.ds(pl.multiple_of(me * er, 8), er), :]
        for d in range(1, n):
            frm = (me + d) % n
            rs_copy(i, frm, frm).wait_recv()
            total = total + rs[i, frm]
        out_ref[0] = total

    grad_pq = back_pair(fq, grad_q[0], grad_q[1])

    scan_run(1)
    rs_begin(0, q_ref, grad_pq)
    scan_end(1)

    grads = []
    for i in range(2):
        g = grad_k[i] + dot3((vh[...], vl[...]), split(prev[1, i, 0:width]), NN)
        grads.append(g + prev[1, i, width:width + 1])
    rs_begin(1, k_ref, back_pair(fk, grads[0], grads[1]))
    rs_finish(0, oq_ref)
    rs_finish(1, ok_ref)

    for d in range(1, nh):
        t1_copy((mh + d) % nh, mh).wait_send()
    for d in range(1, n):
        to = (me + d) % n
        t2_copy(to, me).wait_send()
        rs_copy(0, to, me).wait_send()
        rs_copy(1, to, me).wait_send()


def per_device(n, nh, query_rows, key_rows, value_rows, teacher_out, query_map, key_map, block_map):
    tokens, width = query_rows.shape
    half = query_map.shape[2]
    group = teacher_out.shape[0]
    er = width // n
    br = tokens // n
    rows = width + 8
    chunks = chunk_bounds(rows, 6)
    count = len(chunks)
    vmem = pl.BlockSpec(memory_space=pltpu.VMEM)
    dma = pltpu.SemaphoreType.DMA
    feat = [
        pltpu.VMEM((2, tokens, half), F32),
        pltpu.VMEM((2, tokens, half), BF16),
        pltpu.VMEM((2, tokens, half), BF16),
    ]
    return pl.pallas_call(
        functools.partial(kernel, n, nh, chunks),
        out_shape=(
            jax.ShapeDtypeStruct((1, er, half), F32),
            jax.ShapeDtypeStruct((1, er, half), F32),
        ),
        in_specs=[vmem, vmem, vmem, pl.BlockSpec(memory_space=pl.ANY), vmem, vmem, vmem],
        out_specs=(vmem, vmem),
        scratch_shapes=[
            pltpu.VMEM((group * nh, width), F32),
            pltpu.VMEM((n, br, width), F32),
            pltpu.VMEM((n, br, width), F32),
            pltpu.VMEM((tokens, width), F32),
            pltpu.VMEM((tokens, width), BF16),
            pltpu.VMEM((tokens, width), BF16),
            *feat,
            *feat,
            pltpu.VMEM((2, 2, rows, half), F32),
            pltpu.VMEM((2, rows, half), F32),
            pltpu.VMEM((2, rows, half), F32),
            pltpu.VMEM((2, rows, half), F32),
            pltpu.VMEM((2, rows, half), F32),
            pltpu.VMEM((2, 2, rows, half), F32),
            pltpu.VMEM((2, tokens, half), F32),
            pltpu.VMEM((2, width, half), F32),
            pltpu.VMEM((2, n, er, half), F32),
            dma((2, nh)),
            dma((2, n)),
            dma((2, 2, count)),
            dma((2, 2, count)),
            dma((2, 2, count)),
            dma((2, 2, n)),
            dma((1,)),
        ],
        compiler_params=pltpu.CompilerParams(
            collective_id=0, has_side_effects=True, vmem_limit_bytes=56 * 2**20
        ),
    )(query_rows, key_rows, value_rows, teacher_out,
      query_map.reshape(width, half), key_map.reshape(width, half), block_map)


def solution(mesh):
    placed = (
        P("seq", "head"),
        P("seq", "head"),
        P("seq", "head"),
        P(("seq", "head"), None),
        P("head", None, None),
        P("head", None, None),
        P(),
    )
    return jax.shard_map(
        functools.partial(per_device, mesh.shape["seq"], mesh.shape["head"]),
        mesh=mesh,
        in_specs=placed,
        out_specs=(P("head", "seq", None), P("head", "seq", None)),
        check_vma=False,
    )
```

time: 282 us -> 77.7 us (0.28)
  waiting for transfers between devices: 126 us -> 0 us
  Pallas kernels: 0 us -> 74.9 us
  blocking collectives: 65 us -> 0 us
  matrix products: 31.1 us -> 0 us
  other arithmetic: 18.7 us -> 0 us
  between operations: 14.7 us -> 0.65 us
  local copies, waits for them, and re-layouts: 13.3 us -> 2 us
  starting transfers between devices: 10.8 us -> 0 us
    pallas_call x0 -> x1, Pallas kernels: none -> 74.9 us  [per_device(): pl.pallas_call(functools.partial(kernel, n, nh, chunks), out_shape=(jax.S...]
    unnamed x4 -> x0, waiting for transfers between devices: 69.6 us -> none
    all_gather x2 -> x0, blocking collectives: 65 us -> none  [prefix(): pieces = jax.tree.map(lambda part: lax.all_gather(part, axis), value)]
    all_gather x2 -> x0, waiting for transfers between devices: 48 us -> none  [prefix(): pieces = jax.tree.map(lambda part: lax.all_gather(part, axis), value)]
    dot_general x18 -> x0, matrix products: 31.1 us -> none  [the longest x1 2.97 us: per_device(): grad_fq = jnp.einsum('hts,hsf->htf', weights, feat_k, precision=exact_prec)]
    select_n x29 -> x0, other arithmetic: 17.2 us -> none  [the longest x28 17.2 us: step(): jnp.where(position < mine, new, old)]
    all_to_all x2 -> x0, starting transfers between devices: 10.7 us -> none  [the longest x1 6.46 us: relay_teacher(): lax.all_to_all(by_owner, 'seq', split_axis=0, concat_axis=0, tiled=True)]
    all_to_all x2 -> x0, waiting for transfers between devices: 8.83 us -> none  [the longest x1 8.83 us: relay_teacher(): lax.all_to_all(teacher_out, 'head', split_axis=1, concat_axis=0, tiled=True)]
  transfers between devices with their start and end apart: 5 -> 0, of which waited for: 4 -> 0; matrix products, arithmetic and copies ran while one was open for 8% -> 0% of each run, Pallas kernels for 0% -> 0%
where the time goes in v1:
time: 77.7 us; the launch traced here: 77.5 us
  Pallas kernels  74.9 us (96%)
  local copies, waits for them, and re-layouts  2 us (3%)
    pallas_call x1, Pallas kernels, per_device(): pl.pallas_call(functools.partial(kernel, n, nh, chunks), out_shape=(jax.S...  74.9 us
    unnamed x4, local copies, waits for them, and re-layouts  2 us

profile of v1, /device:TPU:0, one launch (start us, length us, event | category | flops | bytes accessed | tf_op | source)
XLA Modules:
  0.0 77.5 jit_solution(18044315511315770745)
XLA Ops:
  0.6 74.9 %shard_map.86 = (f32[1,32,256]{2,1,0:T(8,128)}, f32[1,32,256]{2,1,0:T(8,128)}) custom-call(f32[512,256]{1,0:T(8,128)} %q_ref.1, f32[512,256]{1,0:T(8,128)} %k_ref.1, f32[512,256]{1,0:T(8,128)} %v_ref.1, f32[128,1024]{1,0:T(8,128)} %t_ref.1, f32[256,256]{1,0:T(8,128)} %bitcast.2, f32[256,256]{1,0:T(8,128)} %bitcast.3, s32[8,8]{1,0:T(8,128)} %bm_ref.1), custom_call_target="tpu_custom_call" | custom-call | tf_op jit(solution)/shard_map/pallas_call | solution.py:360
  75.5 0.0 copy-start
  75.5 1.4 %copy.11 = f32[1,32,256]{2,1,0:T(8,128)} copy(f32[1,32,256]{2,1,0:T(8,128)} %get-tuple-element.4) | data formatting | bytes 65536
  76.9 0.0 copy-done
  76.9 0.6 copy.12
Async XLA Ops:
  75.5 1.4 %copy-start = (f32[1,32,256]{2,1,0:T(8,128)S(1)}, f32[1,32,256]{2,1,0:T(8,128)}, u32[]{:S(2)}) copy-start(f32[1,32,256]{2,1,0:T(8,128)} %get-tuple-element.5) | copy-start | bytes 98308

commit v2 on v1

--- a/solution.py
+++ b/solution.py
@@ -10,6 +10,8 @@
 MESH = pl.DeviceIdType.MESH
 F32 = jnp.float32
 BF16 = jnp.bfloat16
+CH = 11
+EARLY = 3
 NN = (((1,), (0,)), ((), ()))
 NT = (((1,), (1,)), ((), ()))
 TN = (((0,), (0,)), ((), ()))
@@ -193,10 +195,6 @@
     scan_begin(0)
     key_state(c)
 
-    for d in range(1, nh):
-        frm = (mh + d) % nh
-        t1_copy(frm, frm).wait_recv()
-    t1_own.wait()
 
     def t2_copy(to, frm):
         return pltpu.make_async_remote_copy(
@@ -208,8 +206,14 @@
             device_id_type=MESH,
         )
 
-    mine = bm_ref[pl.ds(me, 1), :]
-    for d in range(n):
+    def t2_ready():
+        for d in range(1, nh):
+            frm = (mh + d) % nh
+            t1_copy(frm, frm).wait_recv()
+        t1_own.wait()
+
+    def t2_fill(d):
+        mine = bm_ref[pl.ds(me, 1), :]
         to = (me + d) % n
         held = ((mine >= to * n) & (mine < to * n + n)).astype(F32)
         block = jnp.zeros((br, width), F32)
@@ -219,7 +223,22 @@
             t_arr[me] = block
         else:
             t_send[to] = block
-            t2_copy(to, me).start()
+
+    soon = z < EARLY
+
+    @pl.when(soon)
+    def _():
+        scan_run(0)
+
+    t2_ready()
+    for d in range(n):
+        t2_fill(d)
+        if d > 0:
+            to = (me + d) % n
+
+            @pl.when(soon | (to // inner < z))
+            def _():
+                t2_copy(to, me).start()
 
     features(q_ref, qm_ref, fq, fqh, fql)
     causal = (
@@ -232,7 +251,16 @@
     numerator = dot3(split(scores), (vh[...], vl[...]), NN)
     raw_sum = jnp.sum(scores, axis=-1, keepdims=True)
 
-    scan_run(0)
+    @pl.when(jnp.logical_not(soon))
+    def _():
+        scan_run(0)
+        for d in range(1, n):
+            to = (me + d) % n
+
+            @pl.when(to // inner >= z)
+            def _():
+                t2_copy(to, me).start()
+
     scan_end(0)
 
     for i in range(2):
@@ -280,6 +308,12 @@
     scan_begin(1)
     query_state(c)
 
+    soon_back = outer - 1 - z < EARLY
+
+    @pl.when(soon_back)
+    def _():
+        scan_run(1)
+
     weights = dot3(gn, (vh[...], vl[...]), NT) + grad_div
     w_parts = split(jnp.where(causal, weights, 0.0))
     grad_q = []
@@ -287,7 +321,6 @@
         g = dot3(w_parts, (fkh[i], fkl[i]), NN)
         g = g + dot3(gn, split(prev[0, i, 0:width]), NN)
         grad_q.append(g + grad_div * prev[0, i, width:width + 1])
-        grad_k[i] = dot3(w_parts, (fqh[i], fql[i]), TN)
 
     def back_pair(f, g1, g2):
         p1, p2 = f[0], f[1]
@@ -305,10 +338,8 @@
             device_id_type=MESH,
         )
 
-    def rs_begin(i, rows_ref, grad):
+    def rs_term(i, rows_ref, grad):
         terms[i] = dot3(split(rows_ref[...]), split(grad), TN)
-        for d in range(1, n):
-            rs_copy(i, (me + d) % n, me).start()
 
     def rs_finish(i, out_ref):
         total = terms[i, pl.ds(pl.multiple_of(me * er, 8), er), :]
@@ -318,17 +349,36 @@
             total = total + rs[i, frm]
         out_ref[0] = total
 
-    grad_pq = back_pair(fq, grad_q[0], grad_q[1])
-
-    scan_run(1)
-    rs_begin(0, q_ref, grad_pq)
+    rs_term(0, q_ref, back_pair(fq, grad_q[0], grad_q[1]))
+    for d in range(1, n):
+        to = (me + d) % n
+
+        @pl.when(soon_back | (to // inner > z))
+        def _():
+            rs_copy(0, to, me).start()
+
+    for i in range(2):
+        grad_k[i] = dot3(w_parts, (fqh[i], fql[i]), TN)
+
+    @pl.when(jnp.logical_not(soon_back))
+    def _():
+        scan_run(1)
+        for d in range(1, n):
+            to = (me + d) % n
+
+            @pl.when(to // inner <= z)
+            def _():
+                rs_copy(0, to, me).start()
+
     scan_end(1)
 
     grads = []
     for i in range(2):
         g = grad_k[i] + dot3((vh[...], vl[...]), split(prev[1, i, 0:width]), NN)
         grads.append(g + prev[1, i, width:width + 1])
-    rs_begin(1, k_ref, back_pair(fk, grads[0], grads[1]))
+    rs_term(1, k_ref, back_pair(fk, grads[0], grads[1]))
+    for d in range(1, n):
+        rs_copy(1, (me + d) % n, me).start()
     rs_finish(0, oq_ref)
     rs_finish(1, ok_ref)
 
@@ -348,7 +398,7 @@
     er = width // n
     br = tokens // n
     rows = width + 8
-    chunks = chunk_bounds(rows, 6)
+    chunks = chunk_bounds(rows, CH)
     count = len(chunks)
     vmem = pl.BlockSpec(memory_space=pltpu.VMEM)
     dma = pltpu.SemaphoreType.DMA

time: 77.7 us -> 70.7 us (0.910)
  Pallas kernels: 74.9 us -> 67.9 us
    pallas_call x1, Pallas kernels: 74.9 us -> 67.9 us  [per_device(): pl.pallas_call(functools.partial(kernel, n, nh, chunks), out_shape=(jax.S...]
where the time goes in v2:
time: 70.7 us; the launch traced here: 70.5 us
  Pallas kernels  67.9 us (96%)
  local copies, waits for them, and re-layouts  2 us (3%)
    pallas_call x1, Pallas kernels, per_device(): pl.pallas_call(functools.partial(kernel, n, nh, chunks), out_shape=(jax.S...  67.9 us
    unnamed x4, local copies, waits for them, and re-layouts  2 us

profile of v2, /device:TPU:0, one launch (start us, length us, event | category | flops | bytes accessed | tf_op | source)
XLA Modules:
  0.0 70.5 jit_solution(18416855496517839355)
XLA Ops:
  0.6 67.9 %shard_map.86 = (f32[1,32,256]{2,1,0:T(8,128)}, f32[1,32,256]{2,1,0:T(8,128)}) custom-call(f32[512,256]{1,0:T(8,128)} %q_ref.1, f32[512,256]{1,0:T(8,128)} %k_ref.1, f32[512,256]{1,0:T(8,128)} %v_ref.1, f32[128,1024]{1,0:T(8,128)} %t_ref.1, f32[256,256]{1,0:T(8,128)} %bitcast.2, f32[256,256]{1,0:T(8,128)} %bitcast.3, s32[8,8]{1,0:T(8,128)} %bm_ref.1), custom_call_target="tpu_custom_call" | custom-call | tf_op jit(solution)/shard_map/pallas_call | solution.py:410
  68.5 0.0 copy-start
  68.5 1.4 %copy.11 = f32[1,32,256]{2,1,0:T(8,128)} copy(f32[1,32,256]{2,1,0:T(8,128)} %get-tuple-element.4) | data formatting | bytes 65536
  69.9 0.0 copy-done
  69.9 0.6 copy.12
Async XLA Ops:
  68.5 1.4 %copy-start = (f32[1,32,256]{2,1,0:T(8,128)S(1)}, f32[1,32,256]{2,1,0:T(8,128)}, u32[]{:S(2)}) copy-start(f32[1,32,256]{2,1,0:T(8,128)} %get-tuple-element.5) | copy-start | bytes 98308
